TPU v7x, 32 devices: a whole 2x2x4 slice. The times are simulated.
32 devices in a mesh: row: 8 (over z, x), col: 4 (over y, core).
Axes of the slice: x: 2, y: 2, z: 4, core: 2. Of those that a mesh axis runs over, the one named last changes fastest.
Arguments:
- a_blocks: float32 [8, 4, 8, 128, 128], P('row', 'col'), may hold values from -6 to 6
- a_coords: int32 [8, 4, 2, 8], P('row', 'col'), may hold values from 0 to 63, as said below
- b_blocks: float32 [8, 4, 32, 128, 128], P('row', 'col'), may hold values from -0.5 to 0.5
- b_coords: int32 [8, 4, 2, 32], P('row', 'col'), may hold values from 0 to 31, as said below
Outputs:
- product: float32 [2048, 8192], P('row', 'col')
Inputs may be any that keep to these rules, and one draw needn't show every extreme that they name: `a_coords`: each tile lists 8 distinct block positions, exactly 4 of them in each of its 2 column pieces of 32 block columns, with distinct block columns inside one piece; entry 0 is a block row below 2, entry 1 a block column below 64. `b_coords`: each tile lists 32 distinct block positions; entry 0 is a block row below 32, entry 1 a block column below 16.
All inputs are finite; a program needn't handle non-finite values.
Results may differ from a plain program's by a relative error of at most 0.0003.
Values sent between devices are 32-bit elements; how exact they have to be, the bound alone decides.
No kernel may reach another device: no remote copies, remote signals or barrier semaphores. Data moves between devices by JAX's collectives and lax.ppermute only.
A program may use at most 64 MiB of HBM per device.

v0:
```python
import jax
import jax.numpy as jnp
from jax import lax
from jax.sharding import PartitionSpec as P

BS = 128
KB = 32
RB = 2
CB = 16
STEPS = 2


def passed_along(value, axis, steps):
    count = lax.axis_size(axis)
    pairs = [(source, (source + steps) % count) for source in range(count)]
    return lax.ppermute(value, axis, pairs)


def broadcast(value, axis, source):
    kept = jnp.where(lax.axis_index(axis) == source, value, 0).astype(value.dtype)
    return lax.psum(kept, axis)


def tile_product(a_blk, a_pos, b_blk, b_pos, piece, row_blocks, col_blocks, piece_blocks):
    high = lax.Precision.HIGHEST
    edge = a_blk.shape[1]
    stored = a_blk.shape[0]
    in_piece = a_pos[1] // piece_blocks == piece
    kcol = a_pos[1] % piece_blocks
    match = (kcol[:, None] == b_pos[0][None, :]) & in_piece[:, None]
    which = jnp.sum(jnp.where(match, jnp.arange(stored, dtype=jnp.int32)[:, None], 0), axis=0)
    found = jnp.any(match, axis=0)
    row_of = jnp.sum(jnp.where(match, a_pos[0][:, None], 0), axis=0).astype(jnp.int32)
    picked = jnp.take(a_blk, which, axis=0)
    prods = jnp.einsum("bxy,byz->bxz", picked, b_blk, precision=high)
    rowsel = (
        found[None, :] & (row_of[None, :] == jnp.arange(row_blocks, dtype=jnp.int32)[:, None])
    ).astype(jnp.float32)
    colsel = (b_pos[1][None, :] == jnp.arange(col_blocks, dtype=jnp.int32)[:, None]).astype(
        jnp.float32
    )
    placer = rowsel[:, None, :] * colsel[None, :, :]
    out = jnp.einsum("rcb,bxz->rxcz", placer, prods, precision=high)
    return out.reshape(row_blocks * edge, col_blocks * edge)


def select_piece(blocks, coords, piece, piece_blocks, count):
    inside = (coords[1] // piece_blocks == piece).astype(jnp.int32)
    place = jnp.cumsum(inside) - 1
    picker = (inside[None, :] == 1) & (
        place[None, :] == jnp.arange(count, dtype=jnp.int32)[:, None]
    )
    which = jnp.sum(
        jnp.where(picker, jnp.arange(blocks.shape[0], dtype=jnp.int32)[None, :], 0), axis=1
    )
    chosen = jnp.take(blocks, which, axis=0)
    chosen_pos = jnp.take(coords, which, axis=1)
    return (chosen, chosen_pos)


def per_device(a_blocks, a_coords, b_blocks, b_coords):
    grid_rows = lax.axis_size("row")
    per_col = grid_rows // lax.axis_size("col")
    my_row = lax.axis_index("row")
    own_blocks = a_blocks[0, 0]
    own_pos = a_coords[0, 0]
    sec_blocks = b_blocks[0, 0]
    sec_pos = b_coords[0, 0]
    row_blocks = RB
    col_blocks = CB
    piece_blocks = KB
    total = jnp.zeros((row_blocks * BS, col_blocks * BS), jnp.float32)
    for step in range(STEPS):
        if step > 0:
            sec_blocks, sec_pos = passed_along((sec_blocks, sec_pos), "row", -1)
        piece_row = (my_row + step) % grid_rows
        owner = piece_row // per_col
        half = piece_row % per_col
        count = own_blocks.shape[0] // per_col
        sel_blocks, sel_pos = select_piece(own_blocks, own_pos, half, piece_blocks, count)
        got_blocks, got_pos = (
            broadcast(sel_blocks, "col", owner),
            broadcast(sel_pos, "col", owner),
        )
        total = total + tile_product(
            got_blocks, got_pos, sec_blocks, sec_pos, half, row_blocks, col_blocks, piece_blocks
        )
    return total


def solution(mesh):
    return jax.shard_map(
        per_device,
        mesh=mesh,
        in_specs=(
            P("row", "col", None, None, None),
            P("row", "col", None, None),
            P("row", "col", None, None, None),
            P("row", "col", None, None),
        ),
        out_specs=P("row", "col"),
        check_vma=False,
    )
```

profile of v0, /device:TPU:0, one launch (start us, length us, event | category | flops | bytes accessed | tf_op | source)
XLA Modules:
  0.0 86.0 jit_solution(9201445998355475648)
XLA Ops:
  6.5 0.0 copy-start
  6.5 0.0 copy-start.3
  6.5 0.0 copy-start.2
  6.5 0.0 all-reduce.4.cloned.1.call-start
  6.5 6.0 %collective-permute-start.1 = (f32[32,128,128]{2,1,0:T(8,128)}, f32[32,128,128]{2,1,0:T(8,128)}, u32[]{:S(2)}, u32[]{:S(2)}) collective-permute-start(f32[32,128,128]{2,1,0:T(8,128)} %bitcast.61), channel_id=1, source_target_pairs={{0,28},{4,0},{8,4},{12,8},{16,12},{20,16},{24,20},{28,24},{1,29},{... | collective-permute-start | bytes 6291464 | tf_op jit(solution)/shard_map/ppermute | solution.py:16
  12.6 0.5 collective-permute-start
  13.1 0.7 compare_convert_fusion.2
  13.8 0.7 fusion.32
  14.5 0.2 reduce-window.17
  14.7 0.1 select_reduce_fusion.2
  14.9 0.2 reduce-window.16
  15.0 0.1 select_reduce_fusion.5
  15.2 0.0 copy-done
  15.2 0.6 gather_fusion.3
  15.8 0.6 gather_fusion
  16.4 0.9 %select_select_fusion = (f32[4,128,128]{2,1,0:T(8,128)}, f32[4,128,128]{2,1,0:T(8,128)}) fusion(f32[4,128,128]{2,1,0:T(8,128)S(1)} %gather_fusion.3, pred[4]{0:T(512)(128)(4,1)S(1)} %compare_and_fusion.1, pred[]{:T(512)S(6)} %eq.246, f32[4,128,128]{2,1,0:T(8,128)S(1)} %gather_fusion, pred[4]{0:T(512)(128)(4,1)S(1)} %compare_and_fusion.3, pred[]{:T(512)S(6)} %eq.224), kind=kLoop, calls=%fused_computation.22 | loop fusion | flops 262144 | bytes 1048586 | tf_op jit(solution)/shard_map/jit(_where)/select_n | solution.py:20
  17.3 0.0 all-reduce.4.cloned.1.call-update
  17.4 0.0 copy-done.2
  17.4 0.1 copy.10
  17.5 0.6 gather_fusion.4
  18.0 0.6 gather_fusion.1
  18.6 0.1 bitcast_select_fusion
  18.6 0.1 bitcast_select_fusion.1
  18.7 0.0 copy-done.3
  18.7 5.0 %all-reduce = (s32[2,4]{0,1:T(4,128)S(1)}, s32[2,4]{0,1:T(4,128)S(1)}) all-reduce(s32[2,4]{0,1:T(4,128)S(1)} %bitcast_select_fusion, s32[2,4]{0,1:T(4,128)S(1)} %bitcast_select_fusion.1), channel_id=1, replica_groups=mesh['row'=8,'col'=4] {'col'}, use_global_device_ids=true, to_apply=%region_10.14 | all-reduce | flops 16 | bytes 128 | tf_op jit(solution)/shard_map/psum | solution.py:21
  23.7 0.2 slice_reduce_fusion.2
  23.9 0.2 slice_reduce_fusion
  24.1 33.7 %collective-permute-done = s32[2,32]{1,0:T(2,128)S(1)} collective-permute-done((s32[2,32]{1,0:T(2,128)}, s32[2,32]{1,0:T(2,128)S(1)}, u32[]{:S(2)}, u32[]{:S(2)}) %collective-permute-start) | collective-permute-done | bytes 288 | tf_op jit(solution)/shard_map/ppermute | solution.py:16
  57.8 0.1 fusion.39
  57.9 0.1 select_reduce_fusion
  58.0 0.1 select_reduce_fusion.3
  58.2 0.0 all-reduce.4.cloned.1.call-done
  58.2 0.0 copy-start.1
  58.2 1.7 %gather_fusion.5 = f32[32,128,128]{2,1,0:T(8,128)S(1)} fusion(f32[4,128,128]{2,1,0:T(8,128)} %get-tuple-element.18, s32[1024]{0:T(1024)S(1)} %pad_clamp_fusion), kind=kCustom, calls=%fused_computation.5.clone | custom fusion | bytes 4194432 | tf_op jit(solution)/shard_map/jit(_take)/gather | solution.py:34
  59.9 0.0 copy-done.1
  59.9 2.0 %gather_fusion.2 = f32[32,128,128]{2,1,0:T(8,128)} fusion(f32[4,128,128]{2,1,0:T(8,128)S(1)} %copy-done.1, s32[1024]{0:T(1024)S(1)} %pad_clamp_fusion.2), kind=kCustom, calls=%fused_computation.2.clone | custom fusion | bytes 4194432 | tf_op jit(solution)/shard_map/jit(_take)/gather | solution.py:34
  61.9 4.5 %fusion.8 = f32[32,128,128,1]{2,1,0,3:T(8,128)S(1)} fusion(f32[32,128,128]{2,1,0:T(8,128)} %gather_fusion.2, pred[32]{0:T(512)(128)(4,1)S(1)} %compare_and_fusion.2, f32[1,1,32,128,128]{4,3,2,1,0:T(8,128)} %param.12), kind=kOutput, calls=%fused_computation.16 | convolution fusion | flops 805830656 | bytes 6291488 | tf_op jit(solution)/shard_map/bxy,byz->bxz/dot_general | solution.py:35
  66.4 0.0 collective-permute-done.1
  66.4 3.9 %fusion.11 = f32[32,128,128,1]{2,1,0,3:T(8,128)S(1)} fusion(f32[32,128,128]{2,1,0:T(8,128)} %collective-permute-done.1, f32[32,128,128]{2,1,0:T(8,128)S(1)} %gather_fusion.5, pred[32]{0:T(512)(128)(4,1)S(1)} %compare_and_fusion), kind=kOutput, calls=%fused_computation.17 | convolution fusion | flops 805830656 | bytes 6291488 | tf_op jit(solution)/shard_map/bxy,byz->bxz/dot_general | solution.py:35
  70.3 3.2 %fusion = f32[128,128,2,16]{1,3,2,0:T(8,128)S(1)} fusion(f32[32,128,128,1]{2,1,0,3:T(8,128)S(1)} %fusion.11, f32[16,32]{1,0:T(8,128)S(1)} %fusion.29, f32[2,32]{1,0:T(2,128)S(1)} %and_convert_fusion), kind=kOutput, calls=%fused_computation.7 | convolution fusion | flops 201327616 | bytes 4196608 | tf_op jit(solution)/shard_map/rcb,bxz->rxcz/dot_general | solution.py:43
  73.5 3.2 %add_bitcast_fusion = f32[2,128,16,128]{3,2,0,1:T(8,128)S(1)} fusion(f32[128,128,2,16]{1,3,2,0:T(8,128)S(1)} %fusion, f32[32,128,128,1]{2,1,0,3:T(8,128)S(1)} %fusion.8, f32[16,32]{1,0:T(8,128)S(1)} %fusion.28, f32[2,32]{1,0:T(2,128)S(1)} %and_convert_fusion.1), kind=kOutput, calls=%fused_computation.15 | convolution fusion | flops 201851904 | bytes 6293760 | tf_op jit(solution)/shard_map/rcb,bxz->rxcz/dot_general | solution.py:43
  76.8 0.2 copy.14
  76.9 2.2 %copy.29 = f32[32,8,16,128]{3,1,2,0:T(8,128)} copy(f32[32,8,16,128]{3,2,1,0:T(8,128)S(1)} %bitcast.60) | data formatting | bytes 4194304
  (26 shorter events, 0.2 us)
Async XLA Ops:
  6.5 8.7 %copy-start = (f32[1,1,8,128,128]{4,3,2,1,0:T(8,128)S(1)}, f32[1,1,8,128,128]{4,3,2,1,0:T(8,128)}, u32[]{:S(2)}) copy-start(f32[1,1,8,128,128]{4,3,2,1,0:T(8,128)} %param.10) | copy-start | bytes 1572868
  6.5 12.2 %copy-start.3 = (s32[1,1,2,32]{3,2,1,0:T(2,128)S(1)}, s32[1,1,2,32]{3,2,1,0:T(2,128)}, u32[]{:S(2)}) copy-start(s32[1,1,2,32]{3,2,1,0:T(2,128)} %param.13) | copy-start | bytes 772
  6.5 10.8 %copy-start.2 = (s32[1,1,2,8]{3,2,1,0:T(2,128)S(1)}, s32[1,1,2,8]{3,2,1,0:T(2,128)}, u32[]{:S(2)}) copy-start(s32[1,1,2,8]{3,2,1,0:T(2,128)} %param.11) | copy-start | bytes 196
  6.5 51.6 %all-reduce.4.cloned.1.call-start = ((), (), s32[]{:S(2)}) async-start(), calls=%async_computation | async-start | bytes 1048576 | tf_op jit(solution)/shard_map/psum | solution.py:21
  6.5 59.8 %collective-permute-start.1 = (f32[32,128,128]{2,1,0:T(8,128)}, f32[32,128,128]{2,1,0:T(8,128)}, u32[]{:S(2)}, u32[]{:S(2)}) collective-permute-start(f32[32,128,128]{2,1,0:T(8,128)} %bitcast.61), channel_id=1, source_target_pairs={{0,28},{4,0},{8,4},{12,8},{16,12},{20,16},{24,20},{28,24},{1,29},{... | collective-permute-start | bytes 6291464 | tf_op jit(solution)/shard_map/ppermute | solution.py:16
  12.6 45.2 %collective-permute-start = (s32[2,32]{1,0:T(2,128)}, s32[2,32]{1,0:T(2,128)S(1)}, u32[]{:S(2)}, u32[]{:S(2)}) collective-permute-start(s32[2,32]{1,0:T(2,128)} %bitcast.63), channel_id=1, source_target_pairs={{0,28},{4,0},{8,4},{12,8},{16,12},{20,16},{24,20},{28,24},{1,29},{... | collective-permute-start | bytes 776 | tf_op jit(solution)/shard_map/ppermute | solution.py:16
  58.2 1.7 %copy-start.1 = (f32[4,128,128]{2,1,0:T(8,128)S(1)}, f32[4,128,128]{2,1,0:T(8,128)}, u32[]{:S(2)}) copy-start(f32[4,128,128]{2,1,0:T(8,128)} %get-tuple-element.19) | copy-start | bytes 786436
Sparse Core Ops, SparseCore 0:
  17.5 31.5 all-reduce.3
where the time goes:
time: 86.2 us; the launch traced here: 86 us
  waiting for transfers between devices  33.7 us (39%)
  matrix products  14.8 us (17%)
  between operations  13.7 us (16%)
  local copies, waits for them, and re-layouts  8.72 us (10%)
  starting transfers between devices  6.57 us (8%)
  blocking collectives  4.95 us (6%)
  other arithmetic  3.47 us (4%)
    ppermute x2, waiting for transfers between devices, passed_along(): return lax.ppermute(value, axis, pairs)  33.7 us
    dot_general x2, matrix products, tile_product(): prods = jnp.einsum('bxy,byz->bxz', picked, b_blk, precision=high)  8.36 us
    ppermute x2, starting transfers between devices, passed_along(): return lax.ppermute(value, axis, pairs)  6.56 us
    dot_general x2, matrix products, tile_product(): out = jnp.einsum('rcb,bxz->rxcz', placer, prods, precision=high)  6.46 us
    psum x1, blocking collectives, broadcast(): return lax.psum(kept, axis)  4.95 us
    gather x2, local copies, waits for them, and re-layouts, tile_product(): picked = jnp.take(a_blk, which, axis=0)  3.67 us
    unnamed x9, local copies, waits for them, and re-layouts  2.21 us
  transfers between devices with their start and end apart: 3, of which 1 were waited for; matrix products, arithmetic and copies ran while one was open for 17% of the time, Pallas kernels for 0%

commit v1 on v0

v1 whole, which is shorter than its diff:
```python
import functools

import jax
import jax.numpy as jnp
from jax import lax
from jax.experimental import pallas as pl
from jax.experimental.pallas import tpu as pltpu
from jax.sharding import PartitionSpec as P

KB = 32
RB = 2
CB = 16
STEPS = 2
CHUNKS = (32,)
NOTE = 8

VMEM = pl.BlockSpec(memory_space=pltpu.VMEM)
SMEM = pl.BlockSpec(memory_space=pltpu.SMEM)


def pack_kernel(count, halves_ref, pos_ref, a_ref, *out_refs):
    stored, edge = a_ref.shape[0], a_ref.shape[1]
    lane = lax.broadcasted_iota(jnp.int32, (NOTE, edge), 1)
    line = lax.broadcasted_iota(jnp.int32, (NOTE, edge), 0)
    for s, out in enumerate(out_refs):
        half = halves_ref[s]
        place = jnp.int32(0)
        note = jnp.zeros((NOTE, edge), jnp.int32)
        for m in range(stored):
            row, col = pos_ref[0, m], pos_ref[1, m]
            mine = (col // KB == half) & (place < count)
            at = place

            @pl.when(mine)
            def _():
                out[pl.ds(pl.multiple_of(at * edge, edge), edge), :] = a_ref[m]

            hit = mine & (lane == at)
            note = jnp.where(hit & (line == 0), row, note)
            note = jnp.where(hit & (line == 1), col % KB, note)
            place = place + mine.astype(jnp.int32)
        out[pl.ds(count * edge, NOTE), :] = note.astype(jnp.float32)


def pack(halves, pos, blocks, count):
    edge = blocks.shape[1]
    shape = jax.ShapeDtypeStruct((count * edge + NOTE, edge), jnp.float32)
    return pl.pallas_call(
        functools.partial(pack_kernel, count),
        out_shape=(shape,) * STEPS,
        in_specs=[SMEM, SMEM, VMEM],
        out_specs=(VMEM,) * STEPS,
        compiler_params=pltpu.CompilerParams(vmem_limit_bytes=16 << 20),
        cost_estimate=pl.CostEstimate(flops=0, bytes_accessed=4 * blocks.size * 4, transcendentals=0),
    )(halves, pos, blocks)


def split(x):
    high = x.astype(jnp.bfloat16)
    return high, (x - high.astype(jnp.float32)).astype(jnp.bfloat16)


def dot3(a, b):
    ah, al = split(a)
    bh, bl = split(b)
    dot = functools.partial(jnp.dot, preferred_element_type=jnp.float32)
    return dot(ah, bh) + (dot(ah, bl) + dot(al, bh))


def add_kernel(count, first, has_total, a_pos_ref, b_pos_ref, a_ref, b_ref, *refs):
    out_ref, lut = refs[-2], refs[-1]
    edge = b_ref.shape[1]
    if has_total:
        out_ref[...] = refs[0][...]
    else:
        out_ref[...] = jnp.zeros_like(out_ref)

    @pl.loop(0, KB)
    def _(k):
        lut[k] = -1

    for m in range(count):
        lut[a_pos_ref[1, m]] = m

    @pl.loop(0, b_ref.shape[0])
    def _(m):
        which = lut[b_pos_ref[0, first + m]]

        @pl.when(which >= 0)
        def _():
            row = pl.multiple_of(a_pos_ref[0, which] * edge, edge)
            col = pl.multiple_of(b_pos_ref[1, first + m] * edge, edge)
            at = pl.multiple_of(which * edge, edge)
            part = dot3(a_ref[pl.ds(at, edge), :], b_ref[m])
            out_ref[pl.ds(row, edge), pl.ds(col, edge)] += part


def add_products(piece, piece_pos, b, b_pos, first, total):
    edge = b.shape[1]
    count = piece_pos.shape[1]
    shape = jax.ShapeDtypeStruct((RB * edge, CB * edge), jnp.float32)
    extra = () if total is None else (total,)
    return pl.pallas_call(
        functools.partial(add_kernel, count, first, total is not None),
        out_shape=shape,
        in_specs=[SMEM, SMEM, VMEM, VMEM] + [VMEM] * len(extra),
        out_specs=VMEM,
        scratch_shapes=[pltpu.SMEM((KB,), jnp.int32)],
        compiler_params=pltpu.CompilerParams(vmem_limit_bytes=24 << 20),
        cost_estimate=pl.CostEstimate(
            flops=6 * b.size * edge, bytes_accessed=4 * (b.size + 2 * shape.size), transcendentals=0
        ),
    )(piece_pos, b_pos, piece, b, *extra)


def per_device(a_blocks, a_coords, b_blocks, b_coords):
    rows, cols = lax.axis_size("row"), lax.axis_size("col")
    per_col = rows // cols
    my_row, my_col = lax.axis_index("row"), lax.axis_index("col")
    a, a_pos, b, b_pos = a_blocks[0, 0], a_coords[0, 0], b_blocks[0, 0], b_coords[0, 0]
    count = a.shape[0] // per_col
    edge = a.shape[1]

    back = [((r + 1) % rows, r) for r in range(rows)]
    ring = functools.partial(lax.ppermute, axis_name="row", perm=back)
    starts = [sum(CHUNKS[:k]) for k in range(len(CHUNKS))]
    next_b = [ring(b[s : s + n]) for s, n in zip(starts, CHUNKS, strict=True)]
    next_pos = ring(b_pos)

    halves = jnp.stack([(my_row + s) % rows % per_col for s in range(STEPS)]).astype(jnp.int32)
    packed = pack(halves, a_pos, a, count)
    pieces, piece_pos = [], []
    for s in range(STEPS):
        owner = (my_row + s) % rows // per_col
        got = jnp.where(my_col == owner, packed[s], 0.0)
        for d in range(1, cols):
            pairs = []
            for r in range(rows):
                o = (r + s) % rows // per_col
                pairs.append((r * cols + o, r * cols + (o + d) % cols))
            got = got + lax.ppermute(packed[s], ("row", "col"), pairs)
        pieces.append(got)
        piece_pos.append(got[count * edge : count * edge + 2, :count].astype(jnp.int32))

    total = add_products(pieces[0], piece_pos[0], b, b_pos, 0, None)
    for s, got_b in zip(starts, next_b, strict=True):
        total = add_products(pieces[1], piece_pos[1], got_b, next_pos, s, total)
    return total


def solution(mesh):
    return jax.shard_map(
        per_device,
        mesh=mesh,
        in_specs=(
            P("row", "col", None, None, None),
            P("row", "col", None, None),
            P("row", "col", None, None, None),
            P("row", "col", None, None),
        ),
        out_specs=P("row", "col"),
        check_vma=False,
    )
```

time: 86.2 us -> 58.6 us (0.68)
  the two profiles are of different devices: /device:TPU:0 before, /device:TPU:27 now
where the time goes in v1:
time: 58.6 us
  waiting for transfers between devices  34.1 us (58%)
  Pallas kernels  11.8 us (20%)
  starting transfers between devices  9.42 us (16%)
  local copies, waits for them, and re-layouts  1.9 us (3%)
  other arithmetic  1.18 us (2%)
    ppermute x1, waiting for transfers between devices, per_device(): next_pos = ring(b_pos)  29.6 us
    pallas_call x2, Pallas kernels, add_products(): pl.pallas_call(functools.partial(add_kernel, count, first, total is not N...  11 us
    ppermute x6, starting transfers between devices, per_device(): got = got + lax.ppermute(packed[s], ('row', 'col'), pairs)  5.3 us
    ppermute x6, waiting for transfers between devices, per_device(): got = got + lax.ppermute(packed[s], ('row', 'col'), pairs)  4.52 us
    ppermute x1, starting transfers between devices, per_device(): next_pos = ring(b_pos)  3.87 us
    unnamed x8, local copies, waits for them, and re-layouts  1.9 us
  transfers between devices with their start and end apart: 8, of which 3 were waited for; matrix products, arithmetic and copies ran while one was open for 2% of the time, Pallas kernels for 5%

profile of v1, /device:TPU:27, one launch (start us, length us, event | category | flops | bytes accessed | tf_op | source)
XLA Modules:
  0.0 58.6 jit_solution(6585870048948506278)
XLA Ops:
  0.0 0.0 copy-start
  0.0 0.3 collective-permute-start.4
  0.3 0.1 pad_add_fusion.halves_ref
  0.3 0.0 copy-start.1
  0.3 1.2 %copy-done.1 = f32[1,1,8,128,128]{4,3,2,1,0:T(8,128)S(1)} copy-done((f32[1,1,8,128,128]{4,3,2,1,0:T(8,128)S(1)}, f32[1,1,8,128,128]{4,3,2,1,0:T(8,128)}, u32[]{:S(2)}) %copy-start.1) | copy-done | bytes 524312
  1.5 0.0 copy-start.2
  1.5 0.7 %copy-done.2 = s32[1,1,2,8]{3,2,1,0:T(2,128)S(1)} copy-done((s32[1,1,2,8]{3,2,1,0:T(2,128)S(1)}, s32[1,1,2,8]{3,2,1,0:T(2,128)}, u32[]{:S(2)}) %copy-start.2) | copy-done | bytes 88
  2.2 0.0 copy-start.3
  2.2 0.8 %shard_map.46 = (f32[520,128]{1,0:T(8,128)S(1)}, f32[520,128]{1,0:T(8,128)S(1)}) custom-call(s32[2]{0:T(128)S(1)} %pad_add_fusion.halves_ref, s32[2,8]{1,0:T(2,128)S(1)} %bitcast.9, f32[8,128,128]{2,1,0:T(8,128)S(1)} %bitcast.8), custom_call_target="tpu_custom_call" | custom-call | bytes 2097152 | tf_op jit(solution)/shard_map/pallas_call | solution.py:48
  3.1 0.7 %collective-permute-start.2 = (f32[520,128]{1,0:T(8,128)S(1)}, f32[520,128]{1,0:T(8,128)S(1)}, u32[]{:S(2)}, u32[]{:S(2)}) collective-permute-start(f32[520,128]{1,0:T(8,128)S(1)} %get-tuple-element.7), channel_id=1, source_target_pairs={{0,3},{5,4},{9,8},{14,13},{18,17},{23,22},{27,26},{28,31}} | collective-permute-start | bytes 798728 | tf_op jit(solution)/shard_map/ppermute | solution.py:141
  3.7 0.7 %collective-permute-start.1 = (f32[520,128]{1,0:T(8,128)S(1)}, f32[520,128]{1,0:T(8,128)S(1)}, u32[]{:S(2)}, u32[]{:S(2)}) collective-permute-start(f32[520,128]{1,0:T(8,128)S(1)} %get-tuple-element.7), channel_id=1, source_target_pairs={{0,2},{5,7},{9,11},{14,12},{18,16},{23,21},{27,25},{28,30}} | collective-permute-start | bytes 798728 | tf_op jit(solution)/shard_map/ppermute | solution.py:141
  4.4 1.3 %collective-permute-start = (f32[520,128]{1,0:T(8,128)S(1)}, f32[520,128]{1,0:T(8,128)}, u32[]{:S(2)}, u32[]{:S(2)}) collective-permute-start(f32[520,128]{1,0:T(8,128)S(1)} %get-tuple-element.7), channel_id=1, source_target_pairs={{0,1},{5,6},{9,10},{14,15},{18,19},{23,20},{27,24},{28,29}} | collective-permute-start | bytes 798728 | tf_op jit(solution)/shard_map/ppermute | solution.py:141
  5.7 0.7 %collective-permute-start.7 = (f32[520,128]{1,0:T(8,128)S(1)}, f32[520,128]{1,0:T(8,128)S(1)}, u32[]{:S(2)}, u32[]{:S(2)}) collective-permute-start(f32[520,128]{1,0:T(8,128)S(1)} %get-tuple-element.8), channel_id=1, source_target_pairs={{0,3},{4,7},{9,8},{13,12},{18,17},{22,21},{27,26},{31,30}} | collective-permute-start | bytes 798728 | tf_op jit(solution)/shard_map/ppermute | solution.py:141
  6.5 0.0 collective-permute-done.2
  6.5 1.3 %collective-permute-start.6 = (f32[520,128]{1,0:T(8,128)S(1)}, f32[520,128]{1,0:T(8,128)S(1)}, u32[]{:S(2)}, u32[]{:S(2)}) collective-permute-start(f32[520,128]{1,0:T(8,128)S(1)} %get-tuple-element.8), channel_id=1, source_target_pairs={{0,2},{4,6},{9,11},{13,15},{18,16},{22,20},{27,25},{31,29}} | collective-permute-start | bytes 798728 | tf_op jit(solution)/shard_map/ppermute | solution.py:141
  7.8 0.0 collective-permute-done.1
  7.8 0.7 %collective-permute-start.5 = (f32[520,128]{1,0:T(8,128)S(1)}, f32[520,128]{1,0:T(8,128)S(1)}, u32[]{:S(2)}, u32[]{:S(2)}) collective-permute-start(f32[520,128]{1,0:T(8,128)S(1)} %get-tuple-element.8), channel_id=1, source_target_pairs={{0,1},{4,5},{9,10},{13,14},{18,19},{22,23},{27,24},{31,28}} | collective-permute-start | bytes 798728 | tf_op jit(solution)/shard_map/ppermute | solution.py:141
  8.5 2.0 %collective-permute-done = f32[520,128]{1,0:T(8,128)} collective-permute-done((f32[520,128]{1,0:T(8,128)S(1)}, f32[520,128]{1,0:T(8,128)}, u32[]{:S(2)}, u32[]{:S(2)}) %collective-permute-start) | collective-permute-done | bytes 266272 | tf_op jit(solution)/shard_map/ppermute | solution.py:141
  10.4 3.9 %collective-permute-start.3 = (s32[2,32]{1,0:T(2,128)}, s32[2,32]{1,0:T(2,128)S(1)}, u32[]{:S(2)}, u32[]{:S(2)}) collective-permute-start(s32[2,32]{1,0:T(2,128)} %bitcast.10), channel_id=1, source_target_pairs={{4,0},{8,4},{12,8},{16,12},{20,16},{24,20},{28,24},{0,28},{5,1},{9... | collective-permute-start | bytes 776 | tf_op jit(solution)/shard_map/ppermute | solution.py:128
  14.3 1.0 %add_add_fusion.1.a_ref = f32[520,128]{1,0:T(8,128)S(1)} fusion(f32[520,128]{1,0:T(8,128)S(1)} %collective-permute-done.2, f32[520,128]{1,0:T(8,128)S(1)} %collective-permute-done.1, f32[520,128]{1,0:T(8,128)} %collective-permute-done, f32[520,128]{1,0:T(8,128)S(1)} %get-tuple-element.7, pred[]{:T(512)S(6)} %eq.13), kind=kLoop, calls=%fused_computation.1 | loop fusion | flops 266240 | bytes 1331201 | tf_op jit(solution)/shard_map/add | solution.py:141
  15.3 0.0 collective-permute-done.7
  15.4 2.5 %collective-permute-done.6 = f32[520,128]{1,0:T(8,128)S(1)} collective-permute-done((f32[520,128]{1,0:T(8,128)S(1)}, f32[520,128]{1,0:T(8,128)S(1)}, u32[]{:S(2)}, u32[]{:S(2)}) %collective-permute-start.6) | collective-permute-done | bytes 266272 | tf_op jit(solution)/shard_map/ppermute | solution.py:141
  17.9 0.0 collective-permute-done.5
  17.9 0.1 add_add_fusion.a_ref
  18.0 0.0 copy-done
  18.0 0.0 copy-done.3
  18.0 1.9 %shard_map.47.refs_0_ = f32[256,2048]{1,0:T(8,128)S(1)} custom-call(s32[2,4]{1,0:T(2,128)S(1)} %slice_convert_fusion.a_pos_ref, s32[2,32]{1,0:T(2,128)S(1)} %bitcast.11, f32[520,128]{1,0:T(8,128)S(1)} %add_add_fusion.a_ref, f32[32,128,128]{2,1,0:T(8,128)S(1)} %bitcast.7), custom_call_target="tpu_custom_call" | custom-call | flops 402653184 | bytes 6291456 | tf_op jit(solution)/shard_map/pallas_call | solution.py:103
  20.0 29.6 %collective-permute-done.3.b_pos_ref = s32[2,32]{1,0:T(2,128)S(1)} collective-permute-done((s32[2,32]{1,0:T(2,128)}, s32[2,32]{1,0:T(2,128)S(1)}, u32[]{:S(2)}, u32[]{:S(2)}) %collective-permute-start.3) | collective-permute-done | bytes 288 | tf_op jit(solution)/shard_map/ppermute | solution.py:128
  49.5 0.0 collective-permute-done.4.b_ref
  49.5 9.1 %shard_map.48 = f32[256,2048]{1,0:T(8,128)} custom-call(s32[2,4]{1,0:T(2,128)S(1)} %slice_convert_fusion.1.a_pos_ref, s32[2,32]{1,0:T(2,128)S(1)} %collective-permute-done.3.b_pos_ref, f32[520,128]{1,0:T(8,128)S(1)} %add_add_fusion.1.a_ref, f32[32,128,128]{2,1,0:T(8,128)} %collective-permute-done.4.b_ref, f32[256,2048]{1,0:T(8,128)S(1)} %shard_map.47.refs_0_), custom_call_target="tpu_custom_call" | custom-call | flops 402653184 | bytes 6291456 | tf_op jit(solution)/shard_map/pallas_call | solution.py:103
  (2 shorter events, 0.0 us)
Async XLA Ops:
  0.0 18.0 %copy-start = (f32[1,1,32,128,128]{4,3,2,1,0:T(8,128)S(1)}, f32[1,1,32,128,128]{4,3,2,1,0:T(8,128)}, u32[]{:S(2)}) copy-start(f32[1,1,32,128,128]{4,3,2,1,0:T(8,128)} %param.6) | copy-start | bytes 6291460
  0.0 49.5 %collective-permute-start.4 = (f32[32,128,128]{2,1,0:T(8,128)}, f32[32,128,128]{2,1,0:T(8,128)}, u32[]{:S(2)}, u32[]{:S(2)}) collective-permute-start(f32[32,128,128]{2,1,0:T(8,128)} %bitcast.6), channel_id=1, source_target_pairs={{4,0},{8,4},{12,8},{16,12},{20,16},{24,20},{28,24},{0,28},{5,1},{9... | collective-permute-start | bytes 6291464 | tf_op jit(solution)/shard_map/ppermute | solution.py:127
  0.3 1.2 %copy-start.1 = (f32[1,1,8,128,128]{4,3,2,1,0:T(8,128)S(1)}, f32[1,1,8,128,128]{4,3,2,1,0:T(8,128)}, u32[]{:S(2)}) copy-start(f32[1,1,8,128,128]{4,3,2,1,0:T(8,128)} %param.4) | copy-start | bytes 1572868
  1.5 0.7 %copy-start.2 = (s32[1,1,2,8]{3,2,1,0:T(2,128)S(1)}, s32[1,1,2,8]{3,2,1,0:T(2,128)}, u32[]{:S(2)}) copy-start(s32[1,1,2,8]{3,2,1,0:T(2,128)} %param.5) | copy-start | bytes 196
  2.2 15.8 %copy-start.3 = (s32[1,1,2,32]{3,2,1,0:T(2,128)S(1)}, s32[1,1,2,32]{3,2,1,0:T(2,128)}, u32[]{:S(2)}) copy-start(s32[1,1,2,32]{3,2,1,0:T(2,128)} %param.7) | copy-start | bytes 772
  3.1 3.4 %collective-permute-start.2 = (f32[520,128]{1,0:T(8,128)S(1)}, f32[520,128]{1,0:T(8,128)S(1)}, u32[]{:S(2)}, u32[]{:S(2)}) collective-permute-start(f32[520,128]{1,0:T(8,128)S(1)} %get-tuple-element.7), channel_id=1, source_target_pairs={{0,3},{5,4},{9,8},{14,13},{18,17},{23,22},{27,26},{28,31}} | collective-permute-start | bytes 798728 | tf_op jit(solution)/shard_map/ppermute | solution.py:141
  3.7 4.0 %collective-permute-start.1 = (f32[520,128]{1,0:T(8,128)S(1)}, f32[520,128]{1,0:T(8,128)S(1)}, u32[]{:S(2)}, u32[]{:S(2)}) collective-permute-start(f32[520,128]{1,0:T(8,128)S(1)} %get-tuple-element.7), channel_id=1, source_target_pairs={{0,2},{5,7},{9,11},{14,12},{18,16},{23,21},{27,25},{28,30}} | collective-permute-start | bytes 798728 | tf_op jit(solution)/shard_map/ppermute | solution.py:141
  4.4 6.0 %collective-permute-start = (f32[520,128]{1,0:T(8,128)S(1)}, f32[520,128]{1,0:T(8,128)}, u32[]{:S(2)}, u32[]{:S(2)}) collective-permute-start(f32[520,128]{1,0:T(8,128)S(1)} %get-tuple-element.7), channel_id=1, source_target_pairs={{0,1},{5,6},{9,10},{14,15},{18,19},{23,20},{27,24},{28,29}} | collective-permute-start | bytes 798728 | tf_op jit(solution)/shard_map/ppermute | solution.py:141
  5.7 9.6 %collective-permute-start.7 = (f32[520,128]{1,0:T(8,128)S(1)}, f32[520,128]{1,0:T(8,128)S(1)}, u32[]{:S(2)}, u32[]{:S(2)}) collective-permute-start(f32[520,128]{1,0:T(8,128)S(1)} %get-tuple-element.8), channel_id=1, source_target_pairs={{0,3},{4,7},{9,8},{13,12},{18,17},{22,21},{27,26},{31,30}} | collective-permute-start | bytes 798728 | tf_op jit(solution)/shard_map/ppermute | solution.py:141
  6.5 11.4 %collective-permute-start.6 = (f32[520,128]{1,0:T(8,128)S(1)}, f32[520,128]{1,0:T(8,128)S(1)}, u32[]{:S(2)}, u32[]{:S(2)}) collective-permute-start(f32[520,128]{1,0:T(8,128)S(1)} %get-tuple-element.8), channel_id=1, source_target_pairs={{0,2},{4,6},{9,11},{13,15},{18,16},{22,20},{27,25},{31,29}} | collective-permute-start | bytes 798728 | tf_op jit(solution)/shard_map/ppermute | solution.py:141
  7.8 10.1 %collective-permute-start.5 = (f32[520,128]{1,0:T(8,128)S(1)}, f32[520,128]{1,0:T(8,128)S(1)}, u32[]{:S(2)}, u32[]{:S(2)}) collective-permute-start(f32[520,128]{1,0:T(8,128)S(1)} %get-tuple-element.8), channel_id=1, source_target_pairs={{0,1},{4,5},{9,10},{13,14},{18,19},{22,23},{27,24},{31,28}} | collective-permute-start | bytes 798728 | tf_op jit(solution)/shard_map/ppermute | solution.py:141
  10.4 39.1 %collective-permute-start.3 = (s32[2,32]{1,0:T(2,128)}, s32[2,32]{1,0:T(2,128)S(1)}, u32[]{:S(2)}, u32[]{:S(2)}) collective-permute-start(s32[2,32]{1,0:T(2,128)} %bitcast.10), channel_id=1, source_target_pairs={{4,0},{8,4},{12,8},{16,12},{20,16},{24,20},{28,24},{0,28},{5,1},{9... | collective-permute-start | bytes 776 | tf_op jit(solution)/shard_map/ppermute | solution.py:128
